TPU v7x, 256 devices: a whole 4x4x8 slice. The times are simulated.
256 devices in a mesh: ia: 4 (over y), ja: 16 (over z, core), ka: 4 (over x).
Axes of the slice: x: 4, y: 4, z: 8, core: 2. Of those that a mesh axis runs over, the one named last changes fastest.
Arguments:
- tensor: bfloat16 [48, 6144, 4096], P('ka', 'ia', 'ja'), may hold values from -6 to 6
- factor_b: bfloat16 [4096, 128], P('ja', 'ia'), may hold values from -1 to 1
- factor_c: bfloat16 [48, 128], P('ka', 'ia'), may hold values from -1 to 1
Outputs:
- factor_a: float32 [6144, 128], P(('ia', 'ja', 'ka'))
All inputs are finite; a program needn't handle non-finite values.
Results may differ from a plain program's by a relative error of at most 0.0003.
Values may be sent and summed in bfloat16 or wider, within the bound.
A program may use at most 64 MiB of HBM per device.

v0:
```python
import jax
import jax.numpy as jnp
from jax import lax
from jax.experimental import pallas as pl
from jax.experimental.pallas import tpu as pltpu
from jax.sharding import PartitionSpec as P

LAMBDA_REG = 0.5
MESH = pl.DeviceIdType.MESH
F32 = jnp.float32
BF16 = jnp.bfloat16
EXACT = lax.Precision.HIGHEST

R = 128
NIA, NJA, NKA = 4, 16, 4
NZ = NJA // 2
RC = R // NIA
KB, IB, JB = 12, 1536, 256
ROWS = IB // (NJA * NKA)
BLOCK = ROWS * NKA
PLANE = NIA * NKA
GROWS = R // PLANE
TERMS = 8
R_AT, M_AT, G_AT = ROWS, ROWS + 8, 2 * ROWS + 8
SURE = 2e-4


def nt(a, b):
    return lax.dot_general(a, b, (((1,), (1,)), ((), ())), preferred_element_type=F32)


def tn(a, b):
    return lax.dot_general(a, b, (((0,), (0,)), ((), ())), preferred_element_type=F32)


def exact(a, b):
    return jnp.dot(a, b, preferred_element_type=F32, precision=EXACT)


def eye():
    i = lax.broadcasted_iota(jnp.int32, (R, R), 0)
    j = lax.broadcasted_iota(jnp.int32, (R, R), 1)
    return (i == j).astype(F32)


def split(a):
    high = a.astype(BF16)
    return high, (a - high.astype(F32)).astype(BF16)


def mul3(a, b):
    dot = lambda u, v: jnp.dot(u, v, preferred_element_type=F32)
    return dot(a[0], b[0]) + (dot(a[0], b[1]) + dot(a[1], b[0]))


def fused(
    t_hbm, bc, pack,
    t_v, gat, bfull, call, gpart, growin, gram,
    psend, precv, own, xin, zown, zin,
    t_sem, in_sem, a_send, a_recv, c_send, c_recv, g_send, g_recv, h_send, h_recv,
    p_send, p_recv, x_send, x_recv, z_send, z_recv, met_z, met_far, met_plane,
):
    ia, ja, ka = lax.axis_index("ia"), lax.axis_index("ja"), lax.axis_index("ka")
    z, core = ja // 2, lax.rem(ja, 2)
    other = 1 - core
    plane = ia * NKA + ka
    left = []

    def at_y(o):
        return (lax.rem(ia + NIA + o, NIA), ja, ka)

    def at_x(o):
        return (ia, ja, lax.rem(ka + NKA + o, NKA))

    def at_z(o, c=core):
        return (ia, 2 * lax.rem(z + NZ + o, NZ) + c, ka)

    def tell(sem, device):
        pl.semaphore_signal(sem, inc=1, device_id=device, device_id_type=MESH)

    def others(me, n):
        return [t + (t >= me).astype(jnp.int32) for t in range(n - 1)]

    keep = pltpu.make_async_copy(bc, gat.at[ia], in_sem)
    keep.start()

    barrier = pltpu.get_barrier_semaphore()
    near = [at_y(o) for o in range(1, NIA)] + [at_z(0, other)]
    near += [at_z(o, c) for o in (1, -1) for c in (core, other)]
    near += [at_x(o) for o in range(1, NKA)]
    for device in near:
        tell(barrier, device)


    def slab_copy(i, c):
        rows = pl.ds(pl.multiple_of((2 * i + c) * BLOCK, BLOCK), BLOCK)
        return pltpu.make_async_copy(
            t_hbm.at[:, rows], t_v.at[:, rows], t_sem.at[jnp.where(c == other, i, NZ + i)]
        )

    loads = [pltpu.make_async_copy(t_hbm.at[k], t_v.at[k], t_sem.at[k]) for k in range(KB)]
    for load in loads:
        load.start(priority=1)

    pl.semaphore_wait(barrier, len(near))
    for y in reversed(others(ia, NIA)):
        pltpu.make_async_remote_copy(
            bc, gat.at[ia], a_send, a_recv, device_id=(y, ja, ka), device_id_type=MESH
        ).start()
    for o in (1, -1):
        tell(met_z, at_z(o))
    for o in range(1, NKA):
        tell(met_plane, at_x(o))
    pl.semaphore_wait(met_z, 2)
    for o in (2, -2):
        tell(met_far, at_z(o))
    keep.wait()
    three = gat.at[0 : NIA - 1]
    pltpu.make_async_copy(three, three, a_recv).wait()
    left.append(pltpu.make_async_copy(three, three, a_send).wait)

    bt = gat[:, 0:RC, :].reshape(R, JB)
    gpart[...] = nt(bt, bt)

    mine = pl.multiple_of(plane * GROWS, GROWS)
    pl.semaphore_wait(met_far, 2)

    growin[ja] = gpart[pl.ds(mine, GROWS), :]
    for to in others(ja, NJA):
        pltpu.make_async_remote_copy(
            growin.at[ja], growin.at[ja], g_send, g_recv,
            device_id=(ia, to, ka), device_id_type=MESH,
        ).start()
    crows = jnp.concatenate([gat[i, RC:, 0:RC].astype(F32) for i in range(NIA)], axis=1)
    call[ka] = crows
    for o in range(1, NKA):
        pltpu.make_async_remote_copy(
            call.at[ka], call.at[ka], c_send, c_recv, device_id=at_x(o), device_id_type=MESH
        ).start()
    left.append(pltpu.make_async_copy(growin.at[1:], growin.at[1:], g_send).wait)
    left.append(pltpu.make_async_copy(call.at[0:3], call.at[0:3], c_send).wait)

    bfull[...] = bt.astype(F32).T.astype(BF16)
    b_all = bfull[...]
    scales = [crows[k : k + 1] for k in range(KB)]

    def contract(rows):
        t = t_v[:, pl.ds(rows, BLOCK), :].reshape(KB * BLOCK, JB)
        products = jnp.dot(t, b_all, preferred_element_type=F32)
        total = products[0:BLOCK] * scales[0]
        for k in range(1, KB):
            total = total + products[k * BLOCK : (k + 1) * BLOCK] * scales[k]
        return total

    def pair_copy(i):
        return pltpu.make_async_remote_copy(
            psend.at[i], precv.at[i], p_send.at[i], p_recv.at[i],
            device_id=(ia, 2 * z + other, ka), device_id_type=MESH,
        )

    def sibling_block(i, carry):
        psend[i] = contract(pl.multiple_of((2 * i + other) * BLOCK, BLOCK))
        pair_copy(i).start()
        return carry

    for load in loads:
        load.wait()
    lax.fori_loop(0, NZ, sibling_block, 0)
    left.append(lambda: [pair_copy(i).wait_send() for i in range(NZ)])

    def own_block(i, carry):
        total = contract(pl.multiple_of((2 * i + core) * BLOCK, BLOCK))
        pair_copy(i).wait_recv()
        own[i] = (total + precv[i]).reshape(NKA, ROWS, R)
        for t, to in enumerate(others(ka, NKA)):
            pltpu.make_async_remote_copy(
                own.at[i, to], xin.at[i, ka - (ka > to).astype(jnp.int32)],
                x_send, x_recv.at[i], device_id=(ia, ja, to), device_id_type=MESH,
            ).start()
        return carry

    lax.fori_loop(0, NZ, own_block, 0)
    left.append(pltpu.make_async_copy(xin, xin, x_send).wait)

    def forward(i, carry):
        pltpu.make_async_copy(xin.at[i], xin.at[i], x_recv.at[i]).wait()
        zown[i] = own[i, ka] + (xin[i, 0] + xin[i, 1] + xin[i, 2])

        @pl.when(i != z)
        def _():
            pltpu.make_async_remote_copy(
                zown.at[i], zin.at[z], z_send, z_recv,
                device_id=(ia, 2 * i + core, ka), device_id_type=MESH,
            ).start()

        return carry

    pltpu.make_async_copy(growin.at[1:], growin.at[1:], g_recv).wait()
    rows = growin[0]
    for o in range(1, NJA):
        rows = rows + growin[o]
    gram[pl.ds(mine, GROWS), :] = rows
    pl.semaphore_wait(met_plane, NKA - 1)
    for p in others(plane, PLANE):
        pltpu.make_async_remote_copy(
            gram.at[pl.ds(mine, GROWS)], gram.at[pl.ds(mine, GROWS)], h_send, h_recv,
            device_id=(p // NKA, ja, lax.rem(p, NKA)), device_id_type=MESH,
        ).start()
    left.append(pltpu.make_async_copy(gram.at[0 : R - GROWS], gram.at[0 : R - GROWS], h_send).wait)
    lax.fori_loop(0, NZ, forward, 0)
    left.append(pltpu.make_async_copy(zin.at[1:], zin.at[1:], z_send).wait)

    pltpu.make_async_copy(gram.at[0 : R - GROWS], gram.at[0 : R - GROWS], h_recv).wait()
    pltpu.make_async_copy(call.at[0:3], call.at[0:3], c_recv).wait()
    every = call[...].reshape(NKA * 16, R).astype(BF16)
    one = eye()
    g = gram[...] * tn(every, every) + LAMBDA_REG * one
    pack[G_AT:, :] = g
    bound = jnp.max(jnp.sum(jnp.abs(g), axis=0, keepdims=True), axis=1, keepdims=True)
    alpha = 2.0 / (bound + LAMBDA_REG)
    e = one - alpha * g
    p = one + e
    for _ in range(TERMS - 1):
        parts = split(e)
        e = mul3(parts, parts)
        p = p + mul3(split(p), split(e))
    inv = alpha * p
    rest = one - exact(g, inv)
    pack[R_AT : R_AT + 8, :] = jnp.broadcast_to(
        jnp.max(jnp.sum(jnp.abs(rest), axis=0, keepdims=True), axis=1, keepdims=True), (8, R)
    )
    inv = inv + mul3(split(inv), split(rest))

    zin[z] = zown[z]
    pltpu.make_async_copy(zin.at[1:], zin.at[1:], z_recv).wait()
    rows = zin[0]
    for o in range(1, NZ):
        rows = rows + zin[o]
    pack[M_AT : M_AT + ROWS, :] = rows
    pack[0:ROWS, :] = exact(rows, inv)
    for wait in left:
        wait()


def finish(pack, out_ref, head, mat, rhs, upper, sem):
    load = pltpu.make_async_copy(pack.at[0:M_AT], head, sem.at[0])
    load.start()
    load.wait()
    sure = jnp.max(head[R_AT:M_AT, :]) < SURE

    @pl.when(sure)
    def _():
        out_ref[...] = head[0:ROWS, :]

    @pl.when(jnp.logical_not(sure))
    def _():
        rhs[...] = jnp.zeros((R, R), F32)
        load_g = pltpu.make_async_copy(pack.at[G_AT:], mat, sem.at[0])
        load_m = pltpu.make_async_copy(pack.at[M_AT:G_AT], rhs.at[0:ROWS], sem.at[1])
        load_g.start()
        load_m.start()
        load_g.wait()
        load_m.wait()
        rhs[...] = rhs[...].T
        down = lax.broadcasted_iota(jnp.int32, (R, 1), 0)
        across = lax.broadcasted_iota(jnp.int32, (1, R), 1)

        def column(a, k):
            return jnp.sum(jnp.where(across == k, a, 0.0), axis=1, keepdims=True)

        def forward(k, carry):
            a = mat[...]
            row = mat[pl.ds(k, 1), :]
            root = jnp.sqrt(jnp.sum(jnp.where(across == k, row, 0.0), axis=1, keepdims=True))
            lrow = jnp.where(across >= k, row / root, 0.0)
            lcol = jnp.where(down > k, column(a, k) / root, 0.0)
            upper[pl.ds(k, 1), :] = lrow
            mat[...] = a - lcol * lrow
            b = rhs[pl.ds(k, 1), :] / root
            rhs[...] = jnp.where(down == k, b, rhs[...] - lcol * b)
            return carry

        lax.fori_loop(0, R, forward, 0)

        def backward(step, carry):
            k = R - 1 - step
            col = column(upper[...], k)
            root = jnp.sum(jnp.where(down == k, col, 0.0), axis=0, keepdims=True)
            x = rhs[pl.ds(k, 1), :] / root
            rhs[...] = jnp.where(
                down == k, x, rhs[...] - jnp.where(down < k, col, 0.0) * x
            )
            return carry

        lax.fori_loop(0, R, backward, 0)
        out_ref[...] = rhs[...].T[0:ROWS]


def body(tensor, factor_b, factor_c):
    vmem = pl.BlockSpec(memory_space=pltpu.VMEM)
    hbm = pl.BlockSpec(memory_space=pltpu.HBM)
    dma, signal = pltpu.SemaphoreType.DMA, pltpu.SemaphoreType.REGULAR
    c_rows = jnp.pad(factor_c, ((0, 16 - KB), (0, JB - RC)))
    both = jnp.concatenate([factor_b.T, c_rows], axis=0)
    pack = pl.pallas_call(
        fused,
        out_shape=jax.ShapeDtypeStruct((G_AT + R, R), F32),
        in_specs=[hbm, pl.BlockSpec(memory_space=pl.ANY)],
        out_specs=vmem,
        scratch_shapes=[
            pltpu.VMEM((KB, IB, JB), BF16),
            pltpu.VMEM((NIA, RC + 16, JB), BF16),
            pltpu.VMEM((JB, R), BF16),
            pltpu.VMEM((NKA, 16, R), F32),
            pltpu.VMEM((R, R), F32),
            pltpu.VMEM((NJA, GROWS, R), F32),
            pltpu.VMEM((R, R), F32),
            pltpu.VMEM((NZ, BLOCK, R), F32),
            pltpu.VMEM((NZ, BLOCK, R), F32),
            pltpu.VMEM((NZ, NKA, ROWS, R), F32),
            pltpu.VMEM((NZ, NKA - 1, ROWS, R), F32),
            pltpu.VMEM((NZ, ROWS, R), F32),
            pltpu.VMEM((NZ, ROWS, R), F32),
            dma((NJA,)),
            dma, dma, dma, dma, dma, dma, dma, dma, dma,
            dma((NZ,)),
            dma((NZ,)),
            dma,
            dma((NZ,)),
            dma, dma,
            signal, signal, signal,
        ],
        compiler_params=pltpu.CompilerParams(
            collective_id=0, has_side_effects=True, vmem_limit_bytes=52 * 1024 * 1024
        ),
    )(tensor, both)
    return pl.pallas_call(
        finish,
        out_shape=jax.ShapeDtypeStruct((ROWS, R), F32),
        in_specs=[hbm],
        out_specs=vmem,
        scratch_shapes=[
            pltpu.VMEM((M_AT, R), F32),
            pltpu.VMEM((R, R), F32),
            pltpu.VMEM((R, R), F32),
            pltpu.VMEM((R, R), F32),
            dma((2,)),
        ],
        compiler_params=pltpu.CompilerParams(vmem_limit_bytes=8 * 1024 * 1024),
    )(pack)


def solution(mesh):
    return jax.shard_map(
        body,
        mesh=mesh,
        in_specs=(P("ka", "ia", "ja"), P("ja", "ia"), P("ka", "ia")),
        out_specs=P(("ia", "ja", "ka"), None),
        check_vma=False,
    )
```

profile of v0, /device:TPU:1, one launch (start us, length us, event | category | flops | bytes accessed | tf_op | source)
XLA Modules:
  0.0 27.1 jit_solution(13043317585644455290)
XLA Ops:
  0.0 0.7 %fusion.1.bc = bf16[48,256]{1,0:T(8,128)(2,1)S(1)} fusion(bf16[12,32]{1,0:T(8,128)(2,1)} %param.5, bf16[32,256]{1,0:T(8,128)(2,1)} %bitcast.1), kind=kLoop, calls=%fused_computation.2 | loop fusion | flops 73728 | bytes 41728 | tf_op jit(solution)/shard_map/concatenate | solution.py:304
  0.7 25.6 %shard_map.37.pack = f32[184,128]{1,0:T(8,128)S(1)} custom-call(bf16[12,1536,256]{2,1,0:T(8,128)(2,1)} %t_hbm.1, bf16[48,256]{1,0:T(8,128)(2,1)S(1)} %fusion.1.bc), custom_call_target="tpu_custom_call" | custom-call | tf_op jit(solution)/shard_map/pallas_call | solution.py:305
  26.3 0.8 %shard_map.38 = f32[24,128]{1,0:T(8,128)} custom-call(f32[184,128]{1,0:T(8,128)S(1)} %shard_map.37.pack), custom_call_target="tpu_custom_call" | custom-call | tf_op jit(solution)/shard_map/pallas_call | solution.py:337
where the time goes:
time: 27.4 us; the launch traced here: 27.1 us
  Pallas kernels  26.3 us (96%)
  other arithmetic  0.74 us (3%)
    pallas_call x1, Pallas kernels, body(): pl.pallas_call(fused, out_shape=jax.ShapeDtypeStruct((G_AT + R, R), F32),...  25.6 us
    pallas_call x1, Pallas kernels, body(): pl.pallas_call(finish, out_shape=jax.ShapeDtypeStruct((ROWS, R), F32), in...  0.76 us
    concatenate x1, other arithmetic, body(): both = jnp.concatenate([factor_b.T, c_rows], axis=0)  0.74 us

commit v1 on v0

--- a/solution.py
+++ b/solution.py
@@ -20,7 +20,7 @@
 BLOCK = ROWS * NKA
 PLANE = NIA * NKA
 GROWS = R // PLANE
-TERMS = 8
+TERMS = 7
 R_AT, M_AT, G_AT = ROWS, ROWS + 8, 2 * ROWS + 8
 SURE = 2e-4
 
@@ -49,8 +49,11 @@
 
 
 def mul3(a, b):
-    dot = lambda u, v: jnp.dot(u, v, preferred_element_type=F32)
-    return dot(a[0], b[0]) + (dot(a[0], b[1]) + dot(a[1], b[0]))
+    both = jnp.concatenate(a, axis=1)
+    twice = jnp.concatenate([b[0], b[0]], axis=0)
+    return jnp.dot(both, twice, preferred_element_type=F32) + jnp.dot(
+        a[0], b[1], preferred_element_type=F32
+    )
 
 
 def fused(
@@ -216,7 +219,10 @@
     one = eye()
     g = gram[...] * tn(every, every) + LAMBDA_REG * one
     pack[G_AT:, :] = g
-    bound = jnp.max(jnp.sum(jnp.abs(g), axis=0, keepdims=True), axis=1, keepdims=True)
+    size = jnp.abs(g)
+    across = jnp.sum(size, axis=0, keepdims=True)
+    down = jnp.sum(size, axis=1, keepdims=True)
+    bound = jnp.max(jnp.sum(size * across, axis=1, keepdims=True) / down, axis=0, keepdims=True)
     alpha = 2.0 / (bound + LAMBDA_REG)
     e = one - alpha * g
     p = one + e

time: 27.4 us -> 27.3 us (level)
  no operation moved by 1% of the time
where the time goes in v1:
time: 27.3 us; the launch traced here: 26.9 us
  Pallas kernels  26.2 us (96%)
  other arithmetic  0.74 us (3%)
    pallas_call x1, Pallas kernels, body(): pl.pallas_call(fused, out_shape=jax.ShapeDtypeStruct((G_AT + R, R), F32),...  25.4 us
    pallas_call x1, Pallas kernels, body(): pl.pallas_call(finish, out_shape=jax.ShapeDtypeStruct((ROWS, R), F32), in...  0.76 us
    concatenate x1, other arithmetic, body(): both = jnp.concatenate([factor_b.T, c_rows], axis=0)  0.74 us

profile of v1, /device:TPU:1, one launch (start us, length us, event | category | flops | bytes accessed | tf_op | source)
XLA Modules:
  0.0 26.9 jit_solution(6148273779510639323)
XLA Ops:
  0.0 0.7 %fusion.1.bc = bf16[48,256]{1,0:T(8,128)(2,1)S(1)} fusion(bf16[12,32]{1,0:T(8,128)(2,1)} %param.5, bf16[32,256]{1,0:T(8,128)(2,1)} %bitcast.1), kind=kLoop, calls=%fused_computation.2 | loop fusion | flops 73728 | bytes 41728 | tf_op jit(solution)/shard_map/concatenate | solution.py:310
  0.7 25.4 %shard_map.37.pack = f32[184,128]{1,0:T(8,128)S(1)} custom-call(bf16[12,1536,256]{2,1,0:T(8,128)(2,1)} %t_hbm.1, bf16[48,256]{1,0:T(8,128)(2,1)S(1)} %fusion.1.bc), custom_call_target="tpu_custom_call" | custom-call | tf_op jit(solution)/shard_map/pallas_call | solution.py:311
  26.2 0.8 %shard_map.38 = f32[24,128]{1,0:T(8,128)} custom-call(f32[184,128]{1,0:T(8,128)S(1)} %shard_map.37.pack), custom_call_target="tpu_custom_call" | custom-call | tf_op jit(solution)/shard_map/pallas_call | solution.py:343

commit v2 on v1

--- a/solution.py
+++ b/solution.py
@@ -18,7 +18,8 @@
 KB, IB, JB = 12, 1536, 256
 ROWS = IB // (NJA * NKA)
 BLOCK = ROWS * NKA
-PLANE = NIA * NKA
+PAIR = 2
+PLANE = NIA * PAIR
 GROWS = R // PLANE
 TERMS = 7
 R_AT, M_AT, G_AT = ROWS, ROWS + 8, 2 * ROWS + 8
@@ -66,7 +67,7 @@
     ia, ja, ka = lax.axis_index("ia"), lax.axis_index("ja"), lax.axis_index("ka")
     z, core = ja // 2, lax.rem(ja, 2)
     other = 1 - core
-    plane = ia * NKA + ka
+    plane = ia * PAIR + lax.rem(ka, PAIR)
     left = []
 
     def at_y(o):
@@ -112,8 +113,7 @@
         ).start()
     for o in (1, -1):
         tell(met_z, at_z(o))
-    for o in range(1, NKA):
-        tell(met_plane, at_x(o))
+    tell(met_plane, (ia, ja, ka + 1 - 2 * lax.rem(ka, PAIR)))
     pl.semaphore_wait(met_z, 2)
     for o in (2, -2):
         tell(met_far, at_z(o))
@@ -203,11 +203,11 @@
     for o in range(1, NJA):
         rows = rows + growin[o]
     gram[pl.ds(mine, GROWS), :] = rows
-    pl.semaphore_wait(met_plane, NKA - 1)
+    pl.semaphore_wait(met_plane, 1)
     for p in others(plane, PLANE):
         pltpu.make_async_remote_copy(
             gram.at[pl.ds(mine, GROWS)], gram.at[pl.ds(mine, GROWS)], h_send, h_recv,
-            device_id=(p // NKA, ja, lax.rem(p, NKA)), device_id_type=MESH,
+            device_id=(p // PAIR, ja, ka // PAIR * PAIR + lax.rem(p, PAIR)), device_id_type=MESH,
         ).start()
     left.append(pltpu.make_async_copy(gram.at[0 : R - GROWS], gram.at[0 : R - GROWS], h_send).wait)
     lax.fori_loop(0, NZ, forward, 0)

time: 27.3 us -> 26.6 us (0.974)
  Pallas kernels: 26.2 us -> 25.6 us
    pallas_call x1, Pallas kernels: 25.4 us -> 24.8 us  [body(): pl.pallas_call(fused, out_shape=jax.ShapeDtypeStruct((G_AT + R, R), F32),...]
where the time goes in v2:
time: 26.6 us; the launch traced here: 26.4 us
  Pallas kernels  25.6 us (96%)
  other arithmetic  0.74 us (3%)
    pallas_call x1, Pallas kernels, body(): pl.pallas_call(fused, out_shape=jax.ShapeDtypeStruct((G_AT + R, R), F32),...  24.8 us
    pallas_call x1, Pallas kernels, body(): pl.pallas_call(finish, out_shape=jax.ShapeDtypeStruct((ROWS, R), F32), in...  0.76 us
    concatenate x1, other arithmetic, body(): both = jnp.concatenate([factor_b.T, c_rows], axis=0)  0.74 us

profile of v2, /device:TPU:1, one launch (start us, length us, event | category | flops | bytes accessed | tf_op | source)
XLA Modules:
  0.0 26.4 jit_solution(7461926420355284511)
XLA Ops:
  0.0 0.7 %fusion.1.bc = bf16[48,256]{1,0:T(8,128)(2,1)S(1)} fusion(bf16[12,32]{1,0:T(8,128)(2,1)} %param.5, bf16[32,256]{1,0:T(8,128)(2,1)} %bitcast.1), kind=kLoop, calls=%fused_computation.2 | loop fusion | flops 73728 | bytes 41728 | tf_op jit(solution)/shard_map/concatenate | solution.py:310
  0.7 24.8 %shard_map.37.pack = f32[184,128]{1,0:T(8,128)S(1)} custom-call(bf16[12,1536,256]{2,1,0:T(8,128)(2,1)} %t_hbm.1, bf16[48,256]{1,0:T(8,128)(2,1)S(1)} %fusion.1.bc), custom_call_target="tpu_custom_call" | custom-call | tf_op jit(solution)/shard_map/pallas_call | solution.py:311
  25.6 0.8 %shard_map.38 = f32[24,128]{1,0:T(8,128)} custom-call(f32[184,128]{1,0:T(8,128)S(1)} %shard_map.37.pack), custom_call_target="tpu_custom_call" | custom-call | tf_op jit(solution)/shard_map/pallas_call | solution.py:343

commit v3 on v2

--- a/solution.py
+++ b/solution.py
@@ -59,7 +59,7 @@
 
 def fused(
     t_hbm, bc, pack,
-    t_v, gat, bfull, call, gpart, growin, gram,
+    t_v, gat, bfull, call, growin, gram,
     psend, precv, own, xin, zown, zin,
     t_sem, in_sem, a_send, a_recv, c_send, c_recv, g_send, g_recv, h_send, h_recv,
     p_send, p_recv, x_send, x_recv, z_send, z_recv, met_z, met_far, met_plane,
@@ -123,12 +123,11 @@
     left.append(pltpu.make_async_copy(three, three, a_send).wait)
 
     bt = gat[:, 0:RC, :].reshape(R, JB)
-    gpart[...] = nt(bt, bt)
 
     mine = pl.multiple_of(plane * GROWS, GROWS)
     pl.semaphore_wait(met_far, 2)
 
-    growin[ja] = gpart[pl.ds(mine, GROWS), :]
+    growin[ja] = nt(gat[ia, pl.ds(pl.multiple_of(lax.rem(ka, PAIR) * GROWS, GROWS), GROWS), :], bt)
     for to in others(ja, NJA):
         pltpu.make_async_remote_copy(
             growin.at[ja], growin.at[ja], g_send, g_recv,
@@ -318,7 +317,6 @@
             pltpu.VMEM((NIA, RC + 16, JB), BF16),
             pltpu.VMEM((JB, R), BF16),
             pltpu.VMEM((NKA, 16, R), F32),
-            pltpu.VMEM((R, R), F32),
             pltpu.VMEM((NJA, GROWS, R), F32),
             pltpu.VMEM((R, R), F32),
             pltpu.VMEM((NZ, BLOCK, R), F32),

time: 26.6 us -> 26.4 us (level)
  no operation moved by 1% of the time
where the time goes in v3:
time: 26.4 us; the launch traced here: 26.2 us
  Pallas kernels  25.5 us (97%)
  other arithmetic  0.74 us (3%)
    pallas_call x1, Pallas kernels, body(): pl.pallas_call(fused, out_shape=jax.ShapeDtypeStruct((G_AT + R, R), F32),...  24.7 us
    pallas_call x1, Pallas kernels, body(): pl.pallas_call(finish, out_shape=jax.ShapeDtypeStruct((ROWS, R), F32), in...  0.76 us
    concatenate x1, other arithmetic, body(): both = jnp.concatenate([factor_b.T, c_rows], axis=0)  0.74 us

profile of v3, /device:TPU:1, one launch (start us, length us, event | category | flops | bytes accessed | tf_op | source)
XLA Modules:
  0.0 26.2 jit_solution(8947257932678387001)
XLA Ops:
  0.0 0.7 %fusion.1.bc = bf16[48,256]{1,0:T(8,128)(2,1)S(1)} fusion(bf16[12,32]{1,0:T(8,128)(2,1)} %param.5, bf16[32,256]{1,0:T(8,128)(2,1)} %bitcast.1), kind=kLoop, calls=%fused_computation.2 | loop fusion | flops 73728 | bytes 41728 | tf_op jit(solution)/shard_map/concatenate | solution.py:309
  0.7 24.7 %shard_map.37.pack = f32[184,128]{1,0:T(8,128)S(1)} custom-call(bf16[12,1536,256]{2,1,0:T(8,128)(2,1)} %t_hbm.1, bf16[48,256]{1,0:T(8,128)(2,1)S(1)} %fusion.1.bc), custom_call_target="tpu_custom_call" | custom-call | tf_op jit(solution)/shard_map/pallas_call | solution.py:310
  25.5 0.8 %shard_map.38 = f32[24,128]{1,0:T(8,128)} custom-call(f32[184,128]{1,0:T(8,128)S(1)} %shard_map.37.pack), custom_call_target="tpu_custom_call" | custom-call | tf_op jit(solution)/shard_map/pallas_call | solution.py:341
